TPU v7x, 32 devices: a whole 2x2x4 slice. The times are simulated.
32 devices in a mesh: file: 16 (over z, y, core), win: 2 (over x).
Axes of the slice: x: 2, y: 2, z: 4, core: 2. Of those that a mesh axis runs over, the one named last changes fastest.
Arguments:
- raw: bfloat16 [2, 128, 20480], P('win', None, 'file'), may hold values from -60 to 60
- fir_taps: float32 [64], replicated, may hold values from -0.75 to 0.75
- offsets: int32 [2, 16], P('win', 'file'), may hold values from 0 to 9
- vs_index: int32 [64], replicated, may hold values from 0 to 127, as said below
Outputs:
- correlation: float32 [64, 128, 2048], P('win', 'file')
Inputs may be any that keep to these rules, and one draw needn't show every extreme that they name: `vs_index`: virtual source s is one of the channels s * 2 to s * 2 + 1.
All inputs are finite; a program needn't handle non-finite values.
Results may differ from a plain program's by a relative error of at most 0.0063.
Values may be sent and summed in bfloat16 or wider, within the bound.
No kernel may reach another device: no remote copies, remote signals or barrier semaphores. Data moves between devices by JAX's collectives and lax.ppermute only.
A program may use at most 128 MiB of HBM per device.

v0:
```python
import math
import jax
import jax.numpy as jnp
from jax import lax
from jax.sharding import PartitionSpec as P

R = 10
TAPS = 64
TD = 128
SEG = 2048
BAND = 64
VS_DEV = 4
PRECISE = lax.Precision.HIGHEST
EPSILON = 1e-06


def phase_table(height, breadth, period_len):
    row_index = lax.broadcasted_iota(jnp.int32, (height, breadth), 0)
    col_index = lax.broadcasted_iota(jnp.int32, (height, breadth), 1)
    residue = row_index * col_index % period_len
    angles = residue.astype(jnp.float32) * (2.0 * math.pi / period_len)
    return (jnp.cos(angles), jnp.sin(angles))


def forward_spectrum(samples):
    length = samples.shape[-1]
    factor = min(128, length)
    inner = length // factor
    outer = 2 * length // factor
    half_factor = factor // 2
    leading = samples.shape[:-1]
    arranged = samples.astype(jnp.float32).reshape(leading + (inner, factor))
    cos_a, sin_a = phase_table(inner, outer, outer)
    first_re = jnp.einsum("...pa,pm->...ma", arranged, cos_a, precision=PRECISE)
    first_im = -jnp.einsum("...pa,pm->...ma", arranged, sin_a, precision=PRECISE)
    cos_t, sin_t = phase_table(outer, factor, 2 * length)
    twist_re = first_re * cos_t + first_im * sin_t
    twist_im = first_im * cos_t - first_re * sin_t
    cos_b, sin_b = phase_table(factor, half_factor, factor)
    out_re = jnp.einsum("...ma,an->...nm", twist_re, cos_b, precision=PRECISE) + jnp.einsum(
        "...ma,an->...nm", twist_im, sin_b, precision=PRECISE
    )
    out_im = jnp.einsum("...ma,an->...nm", twist_im, cos_b, precision=PRECISE) - jnp.einsum(
        "...ma,an->...nm", twist_re, sin_b, precision=PRECISE
    )
    return (out_re.reshape(leading + (length,)), out_im.reshape(leading + (length,)))


def inverse_lags(cross_re, cross_im):
    length = cross_re.shape[-1]
    factor = min(128, length)
    inner = length // factor
    outer = 2 * length // factor
    half_factor = factor // 2
    leading = cross_re.shape[:-1]
    quarter = jnp.arange(length, dtype=jnp.int32) % 4
    rotate_c = jnp.where(quarter == 0, 1.0, jnp.where(quarter == 2, -1.0, 0.0)).astype(jnp.float32)
    rotate_s = jnp.where(quarter == 1, 1.0, jnp.where(quarter == 3, -1.0, 0.0)).astype(jnp.float32)
    turned_re = (cross_re * rotate_c + cross_im * rotate_s).reshape(leading + (inner, factor))
    turned_im = (cross_im * rotate_c - cross_re * rotate_s).reshape(leading + (inner, factor))
    cos_a, sin_a = phase_table(inner, outer, outer)
    first_re = jnp.einsum("...pa,pm->...ma", turned_re, cos_a, precision=PRECISE) - jnp.einsum(
        "...pa,pm->...ma", turned_im, sin_a, precision=PRECISE
    )
    first_im = jnp.einsum("...pa,pm->...ma", turned_re, sin_a, precision=PRECISE) + jnp.einsum(
        "...pa,pm->...ma", turned_im, cos_a, precision=PRECISE
    )
    cos_t, sin_t = phase_table(outer, factor, 2 * length)
    twist_re = first_re * cos_t - first_im * sin_t
    twist_im = first_re * sin_t + first_im * cos_t
    cos_b, sin_b = phase_table(factor, half_factor, factor)
    lagged = jnp.einsum("...ma,an->...nm", twist_re, cos_b, precision=PRECISE) - jnp.einsum(
        "...ma,an->...nm", twist_im, sin_b, precision=PRECISE
    )
    return lagged.reshape(leading + (length,))


def whiten(spec_re, spec_im):
    length = spec_re.shape[-1]
    leading = spec_re.shape[:-1]
    magnitude = jnp.sqrt(spec_re * spec_re + spec_im * spec_im)
    amplitude = (
        jnp.mean(magnitude.reshape(leading + (length // BAND, BAND)), axis=-1, keepdims=True)
        + EPSILON
    )
    white_re = (spec_re.reshape(leading + (length // BAND, BAND)) / amplitude).reshape(
        leading + (length,)
    )
    white_im = (spec_im.reshape(leading + (length // BAND, BAND)) / amplitude).reshape(
        leading + (length,)
    )
    return (white_re.astype(jnp.bfloat16), white_im.astype(jnp.bfloat16))


def band_matrix(fir_taps, block_width):
    span = R * block_width + TAPS - R
    period_len = span + R
    flipped = fir_taps[::-1].astype(jnp.bfloat16)
    pattern = jnp.concatenate([flipped, jnp.zeros((period_len - TAPS,), jnp.bfloat16)])
    flat = jnp.tile(pattern, block_width)[: block_width * span]
    return flat.reshape(block_width, span).T


def decimate(extended, offset_now, band_taps):
    row_count = extended.shape[0]
    block_width = band_taps.shape[1]
    span = R * (TD - 1) + TAPS
    segment = lax.dynamic_slice_in_dim(extended, offset_now + 1, span, axis=1)
    block_count = TD // block_width
    stride_len = R * block_width
    leading_part = segment[:, : stride_len * block_count].reshape(
        row_count, block_count, stride_len
    )
    trailing = segment[:, stride_len:]
    trailing = jnp.pad(trailing, ((0, 0), (0, stride_len * block_count - trailing.shape[1])))
    trailing = trailing.reshape(row_count, block_count, stride_len)[:, :, : TAPS - R]
    blocks = jnp.concatenate([leading_part, trailing], axis=2)
    result = jnp.einsum("cbi,io->cbo", blocks, band_taps, preferred_element_type=jnp.float32)
    return result.reshape(row_count, TD)


def local(raw, fir_taps, offsets, vs_index):
    samples = raw[0]
    file_count = lax.axis_size("file")
    win_count = lax.axis_size("win")
    band_taps = band_matrix(fir_taps, math.gcd(TD, 128))
    regrouped = lax.all_to_all(samples, "file", split_axis=0, concat_axis=1, tiled=True)
    shifts = lax.all_gather(offsets, "file", axis=1, tiled=True)
    row_count = regrouped.shape[0]
    file_blocks = regrouped.reshape(row_count, file_count, regrouped.shape[1] // file_count)
    previous = jnp.concatenate(
        [
            jnp.zeros((row_count, 1, TAPS), file_blocks.dtype),
            file_blocks[:, :-1, file_blocks.shape[2] - TAPS :],
        ],
        axis=1,
    )
    extended = jnp.concatenate([previous, file_blocks], axis=2)
    pieces = jax.vmap(decimate, in_axes=(1, 0, None), out_axes=1)(extended, shifts[0], band_taps)
    owned = pieces.reshape(row_count, file_count * TD).astype(jnp.bfloat16)
    row_count = owned.shape[0]
    seg_count = owned.shape[1] // SEG
    own_re, own_im = forward_spectrum(owned.reshape(row_count, seg_count, SEG))
    white_re, white_im = whiten(own_re, own_im)
    file_pos = lax.axis_index("file")
    source_rows = (
        lax.dynamic_slice_in_dim(vs_index, file_pos * VS_DEV, VS_DEV) - file_pos * row_count
    )
    source_re, source_im = (
        lax.all_gather(jnp.take(white_re, source_rows, axis=0), "file", axis=0, tiled=True),
        lax.all_gather(jnp.take(white_im, source_rows, axis=0), "file", axis=0, tiled=True),
    )
    own_both = jnp.concatenate([white_re, white_im], axis=1)
    scale_out = 1.0 / math.sqrt(SEG * seg_count * win_count)
    paired = jnp.stack(
        [
            jnp.concatenate([source_re, source_im], axis=1),
            jnp.concatenate([-source_im, source_re], axis=1),
        ],
        axis=1,
    )
    joined = jnp.einsum("cqf,sdqf->scdf", own_both, paired, preferred_element_type=jnp.float32)
    stacked = lax.psum_scatter(
        joined.reshape(joined.shape[0], joined.shape[1], 2 * SEG),
        "win",
        scatter_dimension=0,
        tiled=True,
    )
    return inverse_lags(stacked[..., :SEG], stacked[..., SEG:]) * scale_out


def solution(mesh):
    return jax.shard_map(
        local,
        mesh=mesh,
        in_specs=(P("win", None, "file"), P(), P("win", "file"), P()),
        out_specs=P("win", "file", None),
        check_vma=False,
    )
```

profile of v0, /device:TPU:0, one launch (start us, length us, event | category | flops | bytes accessed | tf_op | source)
XLA Modules:
  0.0 293.7 jit_solution(40036436673634234)
XLA Ops:
  6.5 7.4 %all-to-all-start = ((bf16[16,8,1280]{2,1,0:T(8,128)(2,1)}), bf16[16,8,1280]{2,1,0:T(8,128)(2,1)S(1)}, u32[]{:S(2)}, u32[]{:S(2)}) async-start(bf16[16,8,1280]{2,1,0:T(8,128)(2,1)} %bitcast.144), calls=%async_computation | async-start | bytes 655360 | tf_op jit(solution)/shard_map/all_to_all | solution.py:127
  17.3 12.4 %all-reduce.4 = s32[16]{0:T(128)S(1)} all-reduce(s32[16]{0:T(128)S(1)} %bitcast_dynamic-update-slice_fusion), channel_id=1, replica_groups=mesh['file'=16,'win'=2] {'file'}, use_global_device_ids=true, to_apply=%add.4 | all-reduce | flops 16 | bytes 128
  31.9 29.9 %while.1 = (s32[]{:T(128)}, bf16[16,8,1344]{2,1,0:T(8,128)(2,1)S(1)}, s32[16,3]{0,1:T(4,128)S(1)}, bf16[16,8,1334]{2,1,0:T(8,128)(2,1)S(1)}, s32[]{:T(128)}) while((s32[]{:T(128)}, bf16[16,8,1344]{2,1,0:T(8,128)(2,1)S(1)}, s32[16,3]{0,1:T(4,128)S(1)}, bf16[16,8,1334]{2,1,0:T(8,128)(2,1)S(1)}, s32[]{:T(128)}) %tuple.29), condition=%wide.while_cond, body=%wide.while_body.sunk | while | flops 2 | bytes 45173 | solution.py:108
  32.5 1.3 dynamic-slice_dynamic-update-slice_fusion.2
  34.4 1.3 dynamic-slice_dynamic-update-slice_fusion.2
  41.9 1.3 dynamic-slice_dynamic-update-slice_fusion.2
  47.5 1.3 dynamic-slice_dynamic-update-slice_fusion.2
  53.1 1.3 dynamic-slice_dynamic-update-slice_fusion.2
  67.5 19.4 %all_gather.11 = bf16[64,1,2048]{2,1,0:T(2,128)(2,1)S(1)} all-gather(bf16[4,1,2048]{2,1,0:T(2,128)(2,1)S(1)} %copy.77), channel_id=1, replica_groups=mesh['file'=16,'win'=2] {'file'}, dimensions={0}, use_global_device_ids=true | all-gather | bytes 278528 | tf_op jit(solution)/shard_map/all_gather | solution.py:151
  87.1 19.7 %all_gather.10 = bf16[64,1,2048]{2,1,0:T(2,128)(2,1)S(1)} all-gather(bf16[4,1,2048]{2,1,0:T(2,128)(2,1)S(1)} %copy.75), channel_id=1, replica_groups=mesh['file'=16,'win'=2] {'file'}, dimensions={0}, use_global_device_ids=true | all-gather | bytes 278528 | tf_op jit(solution)/shard_map/all_gather | solution.py:150
  108.2 4.5 %copy.82 = bf16[64,2,2,2048]{0,2,1,3:T(2,128)(2,1)S(1)} copy(bf16[64,2,2,2048]{3,0,2,1:T(8,128)(2,1)} %pad_maximum_fusion) | data formatting | bytes 2097152 | tf_op jit(solution)/shard_map/stack | solution.py:155
  112.7 6.9 %convolution_bitcast_fusion = f32[64,8,2,2048]{0,1,2,3:T(8,128)} fusion(bf16[64,2,2,2048]{0,2,1,3:T(2,128)(2,1)S(1)} %copy.82, bf16[8,2,2048,1]{0,1,3,2:T(2,128)(2,1)S(1)} %copy.91), kind=kOutput, calls=%fused_computation.4 | convolution fusion | flops 8388608 | bytes 9502720 | tf_op jit(solution)/shard_map/cqf,sdqf->scdf/dot_general | solution.py:162
  119.6 17.3 %copy.84 = f32[64,8,2,2048]{3,2,1,0:T(2,128)} copy(f32[64,8,2,2048]{0,1,2,3:T(8,128)} %convolution_bitcast_fusion) | data formatting | bytes 16777216 | tf_op jit(solution)/shard_map/cqf,sdqf->scdf/transpose | solution.py:162
  136.8 11.8 %reshape.235 = f32[64,8,4096]{2,1,0:T(8,128)} reshape(f32[64,8,2,2048]{3,2,1,0:T(2,128)} %copy.84) | data formatting | bytes 16777216 | tf_op jit(solution)/shard_map/reshape | solution.py:164
  148.7 97.1 %reduce-scatter.2.cloned.1.call-done = f32[32,8,4096]{2,1,0:T(8,128)} async-done(((f32[64,8,4096]{2,1,0:T(8,128)}), f32[32,8,4096]{2,1,0:T(8,128)}) %reduce-scatter.2.cloned.1.call-update) | async-done | bytes 4194320 | tf_op jit(solution)/shard_map/reduce_scatter | solution.py:163
  245.8 2.8 subtract_bitcast_fusion
  248.6 3.5 %fusion.20 = f32[32,32,8,128]{3,0,2,1:T(8,128)S(1)} fusion(f32[32,8,16,128]{3,1,2,0:T(8,128)S(1)} %get-tuple-element.29), kind=kOutput, calls=%fused_computation.28 | convolution fusion | flops 201333760 | bytes 6291456 | tf_op jit(solution)/shard_map/...pa,pm->...ma/dot_general | solution.py:62
  252.1 3.7 %fusion.18 = f32[32,32,8,128]{3,0,2,1:T(8,128)S(1)} fusion(f32[32,8,16,128]{3,1,2,0:T(8,128)S(1)} %get-tuple-element.29), kind=kOutput, calls=%fused_computation.26 | convolution fusion | flops 201333760 | bytes 6291456 | tf_op jit(solution)/shard_map/...pa,pm->...ma/dot_general | solution.py:65
  255.8 3.6 %convolution_subtract_fusion = f32[32,32,8,128]{3,0,2,1:T(8,128)S(1)} fusion(f32[32,32,8,128]{3,0,2,1:T(8,128)S(1)} %fusion.20, f32[32,8,16,128]{3,1,2,0:T(8,128)S(1)} %get-tuple-element.28), kind=kOutput, calls=%fused_computation.17 | convolution fusion | flops 202382336 | bytes 10485760 | tf_op jit(solution)/shard_map/...pa,pm->...ma/dot_general | solution.py:62
  259.4 4.2 %convolution_add_fusion = f32[32,32,8,128]{3,0,2,1:T(8,128)S(1)} fusion(f32[32,32,8,128]{3,0,2,1:T(8,128)S(1)} %fusion.18, f32[32,8,16,128]{3,1,2,0:T(8,128)S(1)} %get-tuple-element.28), kind=kOutput, calls=%fused_computation.16 | convolution fusion | flops 202382336 | bytes 10485760 | tf_op jit(solution)/shard_map/...pa,pm->...ma/dot_general | solution.py:65
  263.6 3.5 %fusion = f32[64,32,8,32]{0,3,2,1:T(8,128)S(1)} fusion(f32[32,32,8,128]{3,0,2,1:T(8,128)S(1)} %convolution_add_fusion, f32[32,32,8,128]{3,0,2,1:T(8,128)S(1)} %convolution_subtract_fusion, f32[32,128]{1,0:T(8,128)S(1)} %get-tuple-element.38, f32[32,128]{1,0:T(8,128)S(1)} %get-tuple-element.39), kind=kOutput, calls=%fused_computation.5 | convolution fusion | flops 808566784 | bytes 10518528 | tf_op jit(solution)/shard_map/...ma,an->...nm/dot_general | solution.py:72
  267.1 5.3 %multiply_bitcast_fusion = f32[32,8,64,32]{2,3,1,0:T(8,128)} fusion(f32[64,32,8,32]{0,3,2,1:T(8,128)S(1)} %fusion, f32[32,32,8,128]{3,0,2,1:T(8,128)S(1)} %convolution_add_fusion, f32[32,32,8,128]{3,0,2,1:T(8,128)S(1)} %convolution_subtract_fusion, f32[32,128]{1,0:T(8,128)S(1)} %get-tuple-element.38, f32[32,128]{1,0:T(8,128)S(1)} %get-tuple-element.39), kind=kOutput, calls=%fused_computation.9 | convolution fusion | flops 809615360 | bytes 12615680 | tf_op jit(solution)/shard_map/...ma,an->...nm/dot_general | solution.py:72
  272.4 6.9 %copy.89 = f32[32,8,64,32]{3,2,1,0:T(8,128)} copy(f32[32,8,64,32]{2,3,1,0:T(8,128)} %multiply_bitcast_fusion) | data formatting | bytes 4194304 | tf_op jit(solution)/shard_map/mul | solution.py:169
  279.3 7.5 %mul.267 = f32[32,8,2048]{2,1,0:T(8,128)} reshape(f32[32,8,64,32]{3,2,1,0:T(8,128)} %copy.89) | data formatting | bytes 4194304 | tf_op jit(solution)/shard_map/mul | solution.py:169
  (98 shorter events, 35.5 us)
Async XLA Ops:
  6.5 25.1 %all-to-all-start = ((bf16[16,8,1280]{2,1,0:T(8,128)(2,1)}), bf16[16,8,1280]{2,1,0:T(8,128)(2,1)S(1)}, u32[]{:S(2)}, u32[]{:S(2)}) async-start(bf16[16,8,1280]{2,1,0:T(8,128)(2,1)} %bitcast.144), calls=%async_computation | async-start | bytes 655360 | tf_op jit(solution)/shard_map/all_to_all | solution.py:127
  13.9 231.8 %reduce-scatter.2.cloned.1.call-start = ((), (), s32[]{:S(2)}) async-start(), calls=%async_computation.2 | async-start | bytes 12582912 | tf_op jit(solution)/shard_map/reduce_scatter | solution.py:163
Sparse Core Ops, SparseCore 0:
  148.8 96.9 reduce-scatter.1
where the time goes:
time: 295 us; the launch traced here: 294 us
  waiting for transfers between devices  97.1 us (33%)
  local copies, waits for them, and re-layouts  84.7 us (29%)
  blocking collectives  51.5 us (17%)
  matrix products  33.2 us (11%)
  between operations  14.4 us (5%)
  starting transfers between devices  7.43 us (3%)
  other arithmetic  5.31 us (2%)
    reduce_scatter x1, waiting for transfers between devices, local(): lax.psum_scatter(joined.reshape(joined.shape[0], joined.shape[1], 2 * SEG...  97.1 us
    gather x48, local copies, waits for them, and re-layouts  29.9 us
    all_gather x1, blocking collectives, local(): lax.all_gather(jnp.take(white_re, source_rows, axis=0), 'file', axis=0, t...  19.7 us
    all_gather x1, blocking collectives, local(): lax.all_gather(jnp.take(white_im, source_rows, axis=0), 'file', axis=0, t...  19.4 us
    transpose x1, local copies, waits for them, and re-layouts, local(): jnp.einsum('cqf,sdqf->scdf', own_both, paired, preferred_element_type=jnp...  17.3 us
    mul x2, local copies, waits for them, and re-layouts, local(): return inverse_lags(stacked[..., :SEG], stacked[..., SEG:]) * scale_out  14.4 us
    unnamed x1, blocking collectives  12.4 us
    reshape x1, local copies, waits for them, and re-layouts, local(): joined.reshape(joined.shape[0], joined.shape[1], 2 * SEG)  11.8 us
  transfers between devices with their start and end apart: 2, of which 1 were waited for; matrix products, arithmetic and copies ran while one was open for 2% of the time, Pallas kernels for 0%

commit v1 on v0

--- a/solution.py
+++ b/solution.py
@@ -120,6 +120,25 @@
 
 
 def local(raw, fir_taps, offsets, vs_index):
+
+    def finish_routes_all(work_x, mesh_name):
+        t_next, even, current_arr = (
+            lax.axis_size(mesh_name),
+            lax.axis_index(mesh_name),
+            work_x.shape[0],
+        )
+        raw_out, h_now = (work_x, 1)
+        while h_now < t_next:
+            leaves = []
+            d = 0
+            while d < t_next:
+                leaves.append((d, (d - h_now) % t_next))
+                d = d + 1
+            raw_out = jnp.concatenate([raw_out, lax.ppermute(raw_out, mesh_name, leaves)], 0)
+            h_now = 2 * h_now
+        main = jnp.roll(raw_out, even * current_arr, axis=0)
+        return main
+
     samples = raw[0]
     file_count = lax.axis_size("file")
     win_count = lax.axis_size("win")
@@ -147,7 +166,7 @@
         lax.dynamic_slice_in_dim(vs_index, file_pos * VS_DEV, VS_DEV) - file_pos * row_count
     )
     source_re, source_im = (
-        lax.all_gather(jnp.take(white_re, source_rows, axis=0), "file", axis=0, tiled=True),
+        finish_routes_all(jnp.take(white_re, source_rows, axis=0), mesh_name="file"),
         lax.all_gather(jnp.take(white_im, source_rows, axis=0), "file", axis=0, tiled=True),
     )
     own_both = jnp.concatenate([white_re, white_im], axis=1)

time: 295 us -> 296 us (level)
  blocking collectives: 51.5 us -> 34.6 us
  waiting for transfers between devices: 97.1 us -> 111 us
  local copies, waits for them, and re-layouts: 84.7 us -> 87.8 us
    all_gather x1 -> x0, blocking collectives: 19.7 us -> none  [local(): lax.all_gather(jnp.take(white_re, source_rows, axis=0), 'file', axis=0, t...]
    ppermute x0 -> x4, waiting for transfers between devices: none -> 13.1 us  [finish_routes_all(): lax.ppermute(raw_out, mesh_name, leaves)]
    gather x48, local copies, waits for them, and re-layouts: 29.9 us -> 32.9 us
  transfers between devices with their start and end apart: 2 -> 6, of which waited for: 1 -> 4; matrix products, arithmetic and copies ran while one was open for 2% -> 2% of each run, Pallas kernels for 0% -> 0%
where the time goes in v1:
time: 296 us; the launch traced here: 295 us
  waiting for transfers between devices  111 us (38%)
  local copies, waits for them, and re-layouts  87.8 us (30%)
  blocking collectives  34.6 us (12%)
  matrix products  33.2 us (11%)
  between operations  14.4 us (5%)
  starting transfers between devices  8.48 us (3%)
  other arithmetic  5.4 us (2%)
    reduce_scatter x1, waiting for transfers between devices, local(): lax.psum_scatter(joined.reshape(joined.shape[0], joined.shape[1], 2 * SEG...  97.6 us
    gather x48, local copies, waits for them, and re-layouts  32.9 us
    all_gather x1, blocking collectives, local(): lax.all_gather(jnp.take(white_im, source_rows, axis=0), 'file', axis=0, t...  22.2 us
    transpose x1, local copies, waits for them, and re-layouts, local(): jnp.einsum('cqf,sdqf->scdf', own_both, paired, preferred_element_type=jnp...  17.3 us
    mul x2, local copies, waits for them, and re-layouts, local(): return inverse_lags(stacked[..., :SEG], stacked[..., SEG:]) * scale_out  14.4 us
    ppermute x4, waiting for transfers between devices, finish_routes_all(): lax.ppermute(raw_out, mesh_name, leaves)  13.1 us
    unnamed x1, blocking collectives  12.4 us
    reshape x1, local copies, waits for them, and re-layouts, local(): joined.reshape(joined.shape[0], joined.shape[1], 2 * SEG)  11.8 us
  transfers between devices with their start and end apart: 6, of which 4 were waited for; matrix products, arithmetic and copies ran while one was open for 2% of the time, Pallas kernels for 0%

profile of v1, /device:TPU:0, one launch (start us, length us, event | category | flops | bytes accessed | tf_op | source)
XLA Modules:
  0.0 294.7 jit_solution(6425315265659066422)
XLA Ops:
  6.5 7.4 %all-to-all-start = ((bf16[16,8,1280]{2,1,0:T(8,128)(2,1)}), bf16[16,8,1280]{2,1,0:T(8,128)(2,1)S(1)}, u32[]{:S(2)}, u32[]{:S(2)}) async-start(bf16[16,8,1280]{2,1,0:T(8,128)(2,1)} %bitcast.144), calls=%async_computation | async-start | bytes 655360 | tf_op jit(solution)/shard_map/all_to_all | solution.py:146
  17.3 12.4 %all-reduce.4 = s32[16]{0:T(128)S(1)} all-reduce(s32[16]{0:T(128)S(1)} %bitcast_dynamic-update-slice_fusion), channel_id=1, replica_groups=mesh['file'=16,'win'=2] {'file'}, use_global_device_ids=true, to_apply=%add.4 | all-reduce | flops 16 | bytes 128
  31.9 32.9 %while.1 = (s32[]{:T(128)}, bf16[16,8,1344]{2,1,0:T(8,128)(2,1)S(1)}, s32[16,3]{0,1:T(4,128)S(1)}, bf16[16,8,1334]{2,1,0:T(8,128)(2,1)S(1)}, s32[]{:T(128)}) while((s32[]{:T(128)}, bf16[16,8,1344]{2,1,0:T(8,128)(2,1)S(1)}, s32[16,3]{0,1:T(4,128)S(1)}, bf16[16,8,1334]{2,1,0:T(8,128)(2,1)S(1)}, s32[]{:T(128)}) %tuple.29), condition=%wide.while_cond, body=%wide.while_body.sunk | while | flops 2 | bytes 45173 | solution.py:108
  32.6 1.4 dynamic-slice_dynamic-update-slice_fusion.2
  34.7 1.4 dynamic-slice_dynamic-update-slice_fusion.2
  36.7 1.4 dynamic-slice_dynamic-update-slice_fusion.2
  38.8 1.4 dynamic-slice_dynamic-update-slice_fusion.2
  72.2 22.2 %all_gather.7 = bf16[64,1,2048]{2,1,0:T(2,128)(2,1)S(1)} all-gather(bf16[4,1,2048]{2,1,0:T(2,128)(2,1)S(1)} %copy.98), channel_id=1, replica_groups=mesh['file'=16,'win'=2] {'file'}, dimensions={0}, use_global_device_ids=true | all-gather | bytes 278528 | tf_op jit(solution)/shard_map/all_gather | solution.py:170
  94.7 4.2 %collective-permute-done.2 = bf16[16,1,2048]{2,0,1:T(8,128)(2,1)S(1)} collective-permute-done((bf16[16,1,2048]{2,0,1:T(8,128)(2,1)S(1)}, bf16[16,1,2048]{2,0,1:T(8,128)(2,1)S(1)}, u32[]{:S(2)}, u32[]{:S(2)}) %collective-permute-start.2) | collective-permute-done | bytes 65568 | tf_op jit(solution)/shard_map/ppermute | solution.py:137
  99.7 7.5 %collective-permute-done.3 = bf16[32,1,2048]{2,0,1:T(8,128)(2,1)S(1)} collective-permute-done((bf16[32,1,2048]{2,0,1:T(8,128)(2,1)S(1)}, bf16[32,1,2048]{2,0,1:T(8,128)(2,1)S(1)}, u32[]{:S(2)}, u32[]{:S(2)}) %collective-permute-start.3) | collective-permute-done | bytes 131104 | tf_op jit(solution)/shard_map/ppermute | solution.py:137
  108.6 4.5 %copy.101 = bf16[64,2,2,2048]{0,2,1,3:T(2,128)(2,1)S(1)} copy(bf16[64,2,2,2048]{3,0,2,1:T(8,128)(2,1)} %pad_maximum_fusion) | data formatting | bytes 2097152 | tf_op jit(solution)/shard_map/stack | solution.py:174
  113.2 6.9 %convolution_bitcast_fusion = f32[64,8,2,2048]{0,1,2,3:T(8,128)} fusion(bf16[64,2,2,2048]{0,2,1,3:T(2,128)(2,1)S(1)} %copy.101, bf16[8,2,2048,1]{0,1,3,2:T(2,128)(2,1)S(1)} %copy.110), kind=kOutput, calls=%fused_computation.4 | convolution fusion | flops 8388608 | bytes 9502720 | tf_op jit(solution)/shard_map/cqf,sdqf->scdf/dot_general | solution.py:181
  120.0 17.3 %copy.103 = f32[64,8,2,2048]{3,2,1,0:T(2,128)} copy(f32[64,8,2,2048]{0,1,2,3:T(8,128)} %convolution_bitcast_fusion) | data formatting | bytes 16777216 | tf_op jit(solution)/shard_map/cqf,sdqf->scdf/transpose | solution.py:181
  137.3 11.8 %reshape.235 = f32[64,8,4096]{2,1,0:T(8,128)} reshape(f32[64,8,2,2048]{3,2,1,0:T(2,128)} %copy.103) | data formatting | bytes 16777216 | tf_op jit(solution)/shard_map/reshape | solution.py:183
  149.2 97.6 %reduce-scatter.2.cloned.1.call-done = f32[32,8,4096]{2,1,0:T(8,128)} async-done(((f32[64,8,4096]{2,1,0:T(8,128)}), f32[32,8,4096]{2,1,0:T(8,128)}) %reduce-scatter.2.cloned.1.call-update) | async-done | bytes 4194320 | tf_op jit(solution)/shard_map/reduce_scatter | solution.py:182
  246.8 2.8 subtract_bitcast_fusion
  249.6 3.5 %fusion.20 = f32[32,32,8,128]{3,0,2,1:T(8,128)S(1)} fusion(f32[32,8,16,128]{3,1,2,0:T(8,128)S(1)} %get-tuple-element.29), kind=kOutput, calls=%fused_computation.28 | convolution fusion | flops 201333760 | bytes 6291456 | tf_op jit(solution)/shard_map/...pa,pm->...ma/dot_general | solution.py:62
  253.1 3.7 %fusion.18 = f32[32,32,8,128]{3,0,2,1:T(8,128)S(1)} fusion(f32[32,8,16,128]{3,1,2,0:T(8,128)S(1)} %get-tuple-element.29), kind=kOutput, calls=%fused_computation.26 | convolution fusion | flops 201333760 | bytes 6291456 | tf_op jit(solution)/shard_map/...pa,pm->...ma/dot_general | solution.py:65
  256.8 3.6 %convolution_subtract_fusion = f32[32,32,8,128]{3,0,2,1:T(8,128)S(1)} fusion(f32[32,32,8,128]{3,0,2,1:T(8,128)S(1)} %fusion.20, f32[32,8,16,128]{3,1,2,0:T(8,128)S(1)} %get-tuple-element.28), kind=kOutput, calls=%fused_computation.17 | convolution fusion | flops 202382336 | bytes 10485760 | tf_op jit(solution)/shard_map/...pa,pm->...ma/dot_general | solution.py:62
  260.4 4.2 %convolution_add_fusion = f32[32,32,8,128]{3,0,2,1:T(8,128)S(1)} fusion(f32[32,32,8,128]{3,0,2,1:T(8,128)S(1)} %fusion.18, f32[32,8,16,128]{3,1,2,0:T(8,128)S(1)} %get-tuple-element.28), kind=kOutput, calls=%fused_computation.16 | convolution fusion | flops 202382336 | bytes 10485760 | tf_op jit(solution)/shard_map/...pa,pm->...ma/dot_general | solution.py:65
  264.6 3.5 %fusion = f32[64,32,8,32]{0,3,2,1:T(8,128)S(1)} fusion(f32[32,32,8,128]{3,0,2,1:T(8,128)S(1)} %convolution_add_fusion, f32[32,32,8,128]{3,0,2,1:T(8,128)S(1)} %convolution_subtract_fusion, f32[32,128]{1,0:T(8,128)S(1)} %get-tuple-element.38, f32[32,128]{1,0:T(8,128)S(1)} %get-tuple-element.39), kind=kOutput, calls=%fused_computation.5 | convolution fusion | flops 808566784 | bytes 10518528 | tf_op jit(solution)/shard_map/...ma,an->...nm/dot_general | solution.py:72
  268.1 5.3 %multiply_bitcast_fusion = f32[32,8,64,32]{2,3,1,0:T(8,128)} fusion(f32[64,32,8,32]{0,3,2,1:T(8,128)S(1)} %fusion, f32[32,32,8,128]{3,0,2,1:T(8,128)S(1)} %convolution_add_fusion, f32[32,32,8,128]{3,0,2,1:T(8,128)S(1)} %convolution_subtract_fusion, f32[32,128]{1,0:T(8,128)S(1)} %get-tuple-element.38, f32[32,128]{1,0:T(8,128)S(1)} %get-tuple-element.39), kind=kOutput, calls=%fused_computation.9 | convolution fusion | flops 809615360 | bytes 12615680 | tf_op jit(solution)/shard_map/...ma,an->...nm/dot_general | solution.py:72
  273.4 6.9 %copy.108 = f32[32,8,64,32]{3,2,1,0:T(8,128)} copy(f32[32,8,64,32]{2,3,1,0:T(8,128)} %multiply_bitcast_fusion) | data formatting | bytes 4194304 | tf_op jit(solution)/shard_map/mul | solution.py:188
  280.4 7.5 %mul.268 = f32[32,8,2048]{2,1,0:T(8,128)} reshape(f32[32,8,64,32]{3,2,1,0:T(8,128)} %copy.108) | data formatting | bytes 4194304 | tf_op jit(solution)/shard_map/mul | solution.py:188
  (108 shorter events, 41.8 us)
Async XLA Ops:
  6.5 25.1 %all-to-all-start = ((bf16[16,8,1280]{2,1,0:T(8,128)(2,1)}), bf16[16,8,1280]{2,1,0:T(8,128)(2,1)S(1)}, u32[]{:S(2)}, u32[]{:S(2)}) async-start(bf16[16,8,1280]{2,1,0:T(8,128)(2,1)} %bitcast.144), calls=%async_computation | async-start | bytes 655360 | tf_op jit(solution)/shard_map/all_to_all | solution.py:146
  13.9 232.8 %reduce-scatter.2.cloned.1.call-start = ((), (), s32[]{:S(2)}) async-start(), calls=%async_computation.2 | async-start | bytes 12582912 | tf_op jit(solution)/shard_map/reduce_scatter | solution.py:182
  69.8 1.5 collective-permute-start
  71.3 23.1 %collective-permute-start.1 = (bf16[8,1,2048]{2,0,1:T(8,128)(2,1)S(1)}, bf16[8,1,2048]{2,0,1:T(8,128)(2,1)S(1)}, u32[]{:S(2)}, u32[]{:S(2)}) collective-permute-start(bf16[8,1,2048]{2,0,1:T(8,128)(2,1)S(1)} %pad_maximum_fusion.3), channel_id=1, source_target_pairs={{0,28},{2,30},{4,0},{6,2},{8,4},{10,6},{12,8},{14,10},{16,12},{18,... | collective-permute-start | bytes 98312 | tf_op jit(solution)/shard_map/ppermute | solution.py:137
  94.5 4.4 %collective-permute-start.2 = (bf16[16,1,2048]{2,0,1:T(8,128)(2,1)S(1)}, bf16[16,1,2048]{2,0,1:T(8,128)(2,1)S(1)}, u32[]{:S(2)}, u32[]{:S(2)}) collective-permute-start(bf16[16,1,2048]{2,0,1:T(8,128)(2,1)S(1)} %pad_maximum_fusion.2), channel_id=1, source_target_pairs={{0,24},{2,26},{4,28},{6,30},{8,0},{10,2},{12,4},{14,6},{16,8},{18,... | collective-permute-start | bytes 196616 | tf_op jit(solution)/shard_map/ppermute | solution.py:137
  98.9 8.4 %collective-permute-start.3 = (bf16[32,1,2048]{2,0,1:T(8,128)(2,1)S(1)}, bf16[32,1,2048]{2,0,1:T(8,128)(2,1)S(1)}, u32[]{:S(2)}, u32[]{:S(2)}) collective-permute-start(bf16[32,1,2048]{2,0,1:T(8,128)(2,1)S(1)} %pad_maximum_fusion.1), channel_id=1, source_target_pairs={{0,16},{2,18},{4,20},{6,22},{8,24},{10,26},{12,28},{14,30},{16,0},... | collective-permute-start | bytes 393224 | tf_op jit(solution)/shard_map/ppermute | solution.py:137
Sparse Core Ops, SparseCore 0:
  149.3 97.4 reduce-scatter.1
